TPU v7x, 256 devices: a whole 4x4x8 slice. The times are simulated.
256 devices in a mesh: section: 8 (over y, x_lo), fsdp: 32 (over x_hi, z, core).
Axes of the slice: x: 4 (x_hi: 2, x_lo: 2; x = x_hi * 2 + x_lo), y: 4, z: 8, core: 2. Of those that a mesh axis runs over, the one named last changes fastest.
Arguments:
- hidden: bfloat16 [2, 32, 192, 2048], P(None, 'fsdp'), may hold values from -20 to 20
- pool_states: bfloat16 [256, 128, 512], P('fsdp', 'section'), may hold values from -6 to 6
- neighbour_ids: int32 [2, 32, 3, 2], P(None, 'fsdp'), may hold values from 0 to 255
- batch_order: int32 [2], replicated, may hold values from 0 to 1, each once
- key_weight: bfloat16 [8, 512, 2048], P('section', 'fsdp'), may hold values from -0.25 to 0.25
- value_weight: bfloat16 [8, 512, 2048], P('section', 'fsdp'), may hold values from -0.25 to 0.25
- query_gain: float32 [8, 2048], P('section'), may hold values from 0.5 to 2
Outputs:
- output: bfloat16 [2, 32, 192, 2048], P(None, 'fsdp', None, 'section')
Inputs may be any that keep to these rules, and one draw needn't show every extreme that they name: `batch_order`: each of the 2 micro-batches once.
All inputs are finite; a program needn't handle non-finite values.
Results may differ from a plain program's by a relative error of at most 0.0078.
Values may be sent and summed in bfloat16 or wider, within the bound.
No kernel may reach another device: no remote copies, remote signals or barrier semaphores. Data moves between devices by JAX's collectives and lax.ppermute only.
A program may use at most 192 MiB of HBM per device.

v0:
```python
import functools

import jax
import jax.numpy as jnp
from jax import lax
from jax.experimental import pallas as pl
from jax.experimental.pallas import tpu as pltpu
from jax.sharding import Mesh
from jax.sharding import PartitionSpec as P

HEAD_DIM = 128
SPAN_LEN = 64
LAYERS = 8
FEATURES = 2048
SLICE = 256
ACTIVE = 128
EPSILON = 1e-06
FIRST = SPAN_LEN - 1
EARLY = 6

AXES = ("yh", "yl", "xl", "xh", "z", "c")
SIZES = (2, 2, 2, 2, 8, 2)
SECTION = ("yh", "yl", "xl")
FSDP = ("xh", "z", "c")
SWAP = [(0, 1), (1, 0)]


def swapped(block, axis):
    return lax.ppermute(block, axis, SWAP)


def shifted(block, axis, size, distance):
    return lax.ppermute(block, axis, [(i, (i + distance) % size) for i in range(size)])


def gather(block):
    gathered = lax.all_gather(block.reshape(-1, 512), ("z", "c"), axis=0)
    return gathered.reshape((16,) + block.shape)


def flipped(block, axes):
    last = 4 ** (len(axes) // 2) - 1
    return lax.ppermute(block, axes, [(i, last - i) for i in range(last + 1)])


FLIP_Y = ("yh", "yl")
FLIP_X = ("xl", "xh")


def quad(block):
    axis = ("yl", "xl")
    return [lax.ppermute(block, axis, [(i, i ^ d) for i in range(4)]) for d in (1, 2, 3)]


def after(*groups):
    return lax.optimization_barrier(groups)


def kv_kernel(layer_ref, enc_ref, rows_ref, key_ref, value_ref, held, sems):
    layer = layer_ref[0]
    copies = [
        pltpu.make_async_copy(
            rows_ref.at[4 * part : 4 * part + 4, layer, kv, xh],
            held.at[kv, xh, 4 * part : 4 * part + 4],
            sems.at[kv, xh, part],
        )
        for kv in range(2)
        for xh in range(2)
        for part in range(4)
    ]
    for copy in copies:
        copy.start()
    for copy in copies[:8]:
        copy.wait()

    def tokens(g):
        return enc_ref[:, :, pl.ds(2 * g, 2)].reshape(256, 512)

    def keys(g, carry):
        made = jnp.dot(
            tokens(g), held[0].reshape(512, 512), preferred_element_type=jnp.float32
        )
        key_ref[g] = made.astype(jnp.bfloat16)
        return carry

    lax.fori_loop(0, 3, keys, 0)
    for copy in copies[8:]:
        copy.wait()

    def values(g, carry):
        made = lax.dot_general(
            held[1].reshape(512, 512),
            tokens(g),
            (((0,), (1,)), ((), ())),
            preferred_element_type=jnp.float32,
        )
        value_ref[g] = made.astype(jnp.bfloat16)
        return carry

    lax.fori_loop(0, 3, values, 0)


def make_kv(encoded, rows, layer):
    vmem = pl.BlockSpec(memory_space=pltpu.VMEM)
    return pl.pallas_call(
        kv_kernel,
        out_shape=(
            jax.ShapeDtypeStruct((3, 256, 512), jnp.bfloat16),
            jax.ShapeDtypeStruct((3, 512, 256), jnp.bfloat16),
        ),
        in_specs=[
            pl.BlockSpec(memory_space=pltpu.SMEM),
            vmem,
            pl.BlockSpec(memory_space=pltpu.HBM),
        ],
        out_specs=(vmem, vmem),
        scratch_shapes=[
            pltpu.VMEM((2, 2, 16, 16, 512), jnp.bfloat16),
            pltpu.SemaphoreType.DMA((2, 2, 4)),
        ],
        compiler_params=pltpu.CompilerParams(vmem_limit_bytes=24 << 20),
        cost_estimate=pl.CostEstimate(
            flops=2 * 768 * 512 * 1024, bytes_accessed=4 << 20, transcendentals=0
        ),
        name="kv",
    )(
        jnp.full((1,), layer, jnp.int32),
        encoded,
        pltpu.with_memory_space_constraint(rows, pltpu.HBM),
    )


SPOT = (0, 1, 3, 5, 7, 6, 4, 2)


def choose_kernel(code_ref, *refs):
    blocks, outs, held = refs[:8], refs[8:10], refs[10]
    for at in range(8):
        held[8 * at : 8 * at + 8] = blocks[at][...]
    for which, out in enumerate(outs):

        def copy(entry, carry, which=which, out=out):
            out[entry] = held[code_ref[which, entry]]
            return carry

        lax.fori_loop(0, 24, copy, 0, unroll=4)


def choose(codes, blocks):
    shape = jax.ShapeDtypeStruct((24, 16, 512), jnp.bfloat16)
    vmem = pl.BlockSpec(memory_space=pltpu.VMEM)
    return pl.pallas_call(
        choose_kernel,
        out_shape=(shape, shape),
        in_specs=[pl.BlockSpec(memory_space=pltpu.SMEM)] + [vmem] * 8,
        out_specs=(vmem, vmem),
        scratch_shapes=[pltpu.VMEM((64, 16, 512), jnp.bfloat16)],
        compiler_params=pltpu.CompilerParams(vmem_limit_bytes=16 << 20),
        name="choose",
    )(codes, *blocks)


def layer_kernel(cur_ref, one_ref, s0_ref, s1_ref, s2_ref, s3_ref, key_ref, value_ref, *outs, last):
    heads = [slice(h * HEAD_DIM, (h + 1) * HEAD_DIM) for h in range(4)]
    queries = [cur_ref[rows, :] for rows in heads]
    own_head = (
        lax.broadcasted_iota(jnp.int32, (512, ACTIVE), 0) // HEAD_DIM
        == lax.broadcasted_iota(jnp.int32, (512, ACTIVE), 1)
    )
    single = one_ref[...].astype(jnp.float32)
    queries_one = jnp.where(own_head, single, 0.0).astype(jnp.bfloat16)
    left = lax.broadcasted_iota(jnp.int32, (1, ACTIVE), 1) < SPAN_LEN

    def dot(first, second):
        return jnp.dot(first, second, preferred_element_type=jnp.float32)

    scores = [
        jnp.where(left, dot(key_ref[0, :, rows], query), dot(key_ref[1, :, rows], query))
        for rows, query in zip(heads, queries)
    ]
    scores.append(dot(key_ref[2], queries_one))
    total = s0_ref[...] + s1_ref[...] + s2_ref[...] + s3_ref[...]
    scale = lax.rsqrt(total * (1.0 / FEATURES) + EPSILON) * HEAD_DIM ** (-0.5)
    scales = [scale[0:1]] * 4 + [scale[1:2]]
    grown = [jnp.exp(score * factor) for score, factor in zip(scores, scales)]
    weights = [
        (one * (1.0 / jnp.sum(one, axis=0, keepdims=True))).astype(jnp.bfloat16) for one in grown
    ]
    mixed = [
        jnp.where(left, dot(value_ref[0, rows, :], weight), dot(value_ref[1, rows, :], weight))
        for rows, weight in zip(heads, weights)
    ]
    mixed_one = dot(value_ref[2], weights[4])
    squares = jnp.zeros((1, ACTIVE), jnp.float32)
    for rows, query, update in zip(heads, queries, mixed):
        made = (query.astype(jnp.float32) + update).astype(jnp.bfloat16)
        wide = made.astype(jnp.float32)
        squares = squares + jnp.sum(wide * wide, axis=0, keepdims=True)
        if last:
            outs[0][0:ACTIVE, rows] = wide.T.astype(jnp.bfloat16)
        else:
            outs[0][rows, :] = made
    mixed_one = jnp.sum(jnp.where(own_head, mixed_one, 0.0), axis=1, keepdims=True)
    made = (single + mixed_one).astype(jnp.bfloat16)
    wide = made.astype(jnp.float32)
    if last:
        outs[0][ACTIVE : ACTIVE + 16, :] = wide.T[0:16].astype(jnp.bfloat16)
    else:
        outs[1][...] = made
        outs[2][0:1, :] = squares
        outs[2][1:2, :] = jnp.sum(wide * wide, axis=0, keepdims=True)


def run_layer(current, single, sums, keys, values, last):
    vmem = pl.BlockSpec(memory_space=pltpu.VMEM)
    if last:
        out_shape = [jax.ShapeDtypeStruct((ACTIVE + 16, 512), jnp.bfloat16)]
    else:
        out_shape = [
            jax.ShapeDtypeStruct((512, ACTIVE), jnp.bfloat16),
            jax.ShapeDtypeStruct((512, ACTIVE), jnp.bfloat16),
            jax.ShapeDtypeStruct((2, ACTIVE), jnp.float32),
        ]
    return pl.pallas_call(
        functools.partial(layer_kernel, last=last),
        out_shape=out_shape,
        in_specs=[vmem] * 8,
        out_specs=[vmem] * len(out_shape),
        compiler_params=pltpu.CompilerParams(vmem_limit_bytes=24 << 20),
        cost_estimate=pl.CostEstimate(
            flops=2 * 20 * 256 * 128 * 128, bytes_accessed=2 << 20, transcendentals=5 * 256 * 128
        ),
        name="layer",
    )(current, single, *sums, keys, values)


def rms_scale(values):
    return values * lax.rsqrt(jnp.mean(values * values, axis=-1, keepdims=True) + EPSILON)


def pick(mask, first, second):
    return jnp.where(mask.reshape(mask.shape + (1, 1)), first, second)


def parts_kernel(key_ref, value_ref, gain_ref, out_ref):
    for label in range(2):
        for xl in range(2):
            for half, y in enumerate((label, 3 - label)):
                spot = 2 * y + xl
                source = slice(spot * SLICE, (spot + 1) * SLICE)
                target = slice(half * SLICE, (half + 1) * SLICE)
                keys = key_ref[0, :, source].astype(jnp.float32) * gain_ref[:, source]
                for section in (2 * label + xl, 2 * (3 - label) + xl):
                    out_ref[section, 0, :, target] = keys.astype(jnp.bfloat16)
                    out_ref[section, 1, :, target] = value_ref[0, :, source]


def weight_parts(key_weight, value_weight, query_gain):
    vmem = pl.BlockSpec(memory_space=pltpu.VMEM)
    return pl.pallas_call(
        parts_kernel,
        out_shape=jax.ShapeDtypeStruct((8, 2, 16, 512), jnp.bfloat16),
        in_specs=[vmem] * 3,
        out_specs=vmem,
        name="parts",
    )(key_weight, value_weight, query_gain)


def per_device(
    hidden, pool_states, neighbour_ids, batch_order, key_weight, value_weight, query_gain
):
    place = {axis: lax.axis_index(axis) for axis in AXES}
    yh, yl, xl, xh, z, c = (place[axis] for axis in AXES)

    is_low = xh == 0
    label = yl ^ yh

    def both_halves(part, other):
        halves = [jnp.where(is_low, part, other), jnp.where(is_low, other, part)]
        return jnp.stack(halves, axis=2)

    def up(block):
        return shifted(block, "z", 8, 1)

    def down(block):
        return shifted(block, "z", 8, -1)

    parts = weight_parts(key_weight, value_weight, query_gain)
    parts, neighbour_ids = after(parts, neighbour_ids)
    rows = lax.all_to_all(parts, SECTION, 0, 0)
    ids = jnp.take(neighbour_ids[:, 0], batch_order, axis=0, mode="clip").reshape(2, 6)
    own = lax.dynamic_index_in_dim(ids, yh, 0, keepdims=False)
    ids = jnp.concatenate([own, lax.dynamic_index_in_dim(ids, 1 - yh, 0, keepdims=False)])
    ids, pool_states = after(ids, pool_states)
    up_1, down_1 = up(pool_states), down(pool_states)
    up_1, down_1, ids, rows = after(up_1, down_1, ids, rows)

    up_2, down_2 = up(up_1), down(down_1)
    rows = both_halves(rows, swapped(rows, "xh"))
    pair = jnp.stack([ids, swapped(ids, "c")])
    opposite = shifted(pool_states, "z", 8, 4)
    up_2, down_2, pair, rows = after(up_2, down_2, pair, rows)
    block, late = rows[:EARLY], rows[EARLY:]

    up_3, down_3 = up(up_2), down(down_2)
    theirs = jnp.concatenate([pair, flipped(pair, FLIP_X)], axis=1)
    codes = jnp.asarray(SPOT, jnp.int32)[(z - (theirs >> 4)) & 7] * 8 + (theirs & 7)
    up_3, down_3, opposite, codes = after(up_3, down_3, opposite, codes)

    early = gather(block)
    pool = [pool_states, up_1, down_1, up_2, down_2, up_3, down_3, opposite]
    kept, sent = choose(codes, pool)
    both = pick(((theirs[0] >> 3) & 1) == c, kept, swapped(sent, "c")).reshape(4, 6, 16, 512)

    from_y, from_x, from_xy = after(
        *(
            flipped(both[part], axes)
            for part, axes in ((1, FLIP_Y), (2, FLIP_X), (3, FLIP_Y + FLIP_X))
        )
    )
    here = (own >> 7) == xh
    tokens = jnp.stack([pick(here, both[0], from_x), pick(here, from_y, from_xy)])
    tokens = rms_scale(tokens.astype(jnp.float32)).astype(jnp.bfloat16)

    tokens, hidden = after(tokens, hidden)
    encoded = jnp.stack([tokens] + quad(tokens))
    ordered = jnp.take(hidden[:, 0], batch_order, axis=0, mode="clip")
    start = lax.dynamic_index_in_dim(ordered, yh, 0, keepdims=False)[FIRST:]
    wide = start.astype(jnp.float32)
    total = jnp.sum(wide * wide, axis=-1)
    sums = jnp.stack([total[:ACTIVE], jnp.broadcast_to(total[ACTIVE:], (ACTIVE,))])
    mine = jnp.concatenate(
        [
            lax.dynamic_slice_in_dim(start, (2 * y + xl) * SLICE, SLICE, 1)
            for y in (label, 3 - label)
        ],
        axis=1,
    )
    current = mine[:ACTIVE].T
    single = jnp.broadcast_to(mine[ACTIVE][:, None], (512, ACTIVE))
    encoded, sums, current, single = after(encoded, sums, current, single)

    nothing = jnp.zeros_like(sums)
    sums = [sums, nothing, nothing, nothing]
    late = gather(late)
    for layer in range(LAYERS):
        last = layer == LAYERS - 1
        if layer < EARLY:
            keys, values = make_kv(encoded, early, layer)
        else:
            keys, values = make_kv(encoded, late, layer - EARLY)
        outs = run_layer(current, single, sums, keys, values, last)
        if not last:
            current, single, partial = outs
            sums = [partial] + quad(partial)
    finished = outs[0].reshape(ACTIVE + 16, 2, SLICE)
    kept = lax.dynamic_index_in_dim(finished, yh, 1, keepdims=False)
    got = flipped(lax.dynamic_index_in_dim(finished, 1 - yh, 1, keepdims=False), FLIP_Y)
    low = yh == 0
    tails = jnp.stack([jnp.where(low, kept, got), jnp.where(low, got, kept)])[:, : ACTIVE + 1]
    heads = lax.dynamic_slice_in_dim(ordered[:, :FIRST], (yh * 4 + yl * 2 + xl) * SLICE, SLICE, 2)
    return jnp.concatenate([heads, tails], axis=1)[:, None]


def solution(mesh):
    split = Mesh(mesh.devices.reshape(SIZES), AXES)
    in_specs = (
        P(None, FSDP, None, None),
        P(FSDP, SECTION, None),
        P(None, FSDP, None, None),
        P(),
        P(SECTION, FSDP, None),
        P(SECTION, FSDP, None),
        P(SECTION, None),
    )
    out_specs = P(None, FSDP, None, SECTION)
    return jax.shard_map(
        per_device, mesh=split, in_specs=in_specs, out_specs=out_specs, check_vma=False
    )
```

profile of v0, /device:TPU:4, one launch (start us, length us, event | category | flops | bytes accessed | tf_op | source)
XLA Modules:
  0.0 152.3 jit_solution(3422388112055983164)
XLA Ops:
  6.5 1.7 %parts.1 = bf16[8,2,16,512]{3,2,1,0:T(8,128)(2,1)} custom-call(bf16[1,16,2048]{2,1,0:T(8,128)(2,1)} %key_ref.1, bf16[1,16,2048]{2,1,0:T(8,128)(2,1)} %value_ref.1, f32[1,2048]{1,0:T(1,128)} %gain_ref.1), custom_call_target="tpu_custom_call" | custom-call | tf_op jit(solution)/shard_map/parts/pallas_call | solution.py:260
  8.2 5.1 %all-to-all-start = ((bf16[8,2,16,512]{3,2,1,0:T(8,128)(2,1)}), bf16[8,2,16,512]{3,2,1,0:T(8,128)(2,1)S(1)}, u32[]{:S(2)}, u32[]{:S(2)}) async-start(bf16[8,2,16,512]{3,2,1,0:T(8,128)(2,1)} %parts.1), calls=%async_computation | async-start | bytes 524288 | tf_op jit(solution)/shard_map/all_to_all | solution.py:290
  15.6 1.9 %collective-permute-start = (bf16[8,16,512]{2,1,0:T(8,128)(2,1)}, bf16[8,16,512]{2,1,0:T(8,128)(2,1)S(1)}, u32[]{:S(2)}, u32[]{:S(2)}) collective-permute-start(bf16[8,16,512]{2,1,0:T(8,128)(2,1)} %refs_0_), channel_id=1, source_target_pairs={{0,2},{2,4},{4,6},{6,8},{8,10},{10,12},{12,14},{14,0},{1,3},{3,5},... | collective-permute-start | bytes 393224 | tf_op jit(solution)/shard_map/ppermute | solution.py:33
  17.5 4.0 %collective-permute-start.1 = (bf16[8,16,512]{2,1,0:T(8,128)(2,1)}, bf16[8,16,512]{2,1,0:T(8,128)(2,1)S(1)}, u32[]{:S(2)}, u32[]{:S(2)}) collective-permute-start(bf16[8,16,512]{2,1,0:T(8,128)(2,1)} %refs_0_), channel_id=1, source_target_pairs={{0,14},{2,0},{4,2},{6,4},{8,6},{10,8},{12,10},{14,12},{1,15},{3,1}... | collective-permute-start | bytes 393224 | tf_op jit(solution)/shard_map/ppermute | solution.py:33
  21.6 3.3 %collective-permute-done.refs_1_ = bf16[8,16,512]{2,1,0:T(8,128)(2,1)S(1)} collective-permute-done((bf16[8,16,512]{2,1,0:T(8,128)(2,1)}, bf16[8,16,512]{2,1,0:T(8,128)(2,1)S(1)}, u32[]{:S(2)}, u32[]{:S(2)}) %collective-permute-start) | collective-permute-done | bytes 131104 | tf_op jit(solution)/shard_map/ppermute | solution.py:33
  25.7 3.2 %collective-permute-start.3 = (bf16[8,16,512]{2,1,0:T(8,128)(2,1)S(1)}, bf16[8,16,512]{2,1,0:T(8,128)(2,1)S(1)}, u32[]{:S(2)}, u32[]{:S(2)}) collective-permute-start(bf16[8,16,512]{2,1,0:T(8,128)(2,1)S(1)} %collective-permute-done.1.refs_2_), channel_id=1, source_target_pairs={{0,14},{2,0},{4,2},{6,4},{8,6},{10,8},{12,10},{14,12},{1,15},{3,1}... | collective-permute-start | bytes 393224 | tf_op jit(solution)/shard_map/ppermute | solution.py:33
  30.1 3.5 %collective-permute-done.5 = bf16[8,2,16,512]{3,2,1,0:T(8,128)(2,1)S(1)} collective-permute-done((bf16[8,2,16,512]{3,2,1,0:T(8,128)(2,1)S(1)}, bf16[8,2,16,512]{3,2,1,0:T(8,128)(2,1)S(1)}, u32[]{:S(2)}, u32[]{:S(2)}) %collective-permute-start.5) | collective-permute-done | bytes 262176 | tf_op jit(solution)/shard_map/ppermute | solution.py:29
  35.3 4.1 %collective-permute-start.9 = (bf16[8,16,512]{2,1,0:T(8,128)(2,1)S(1)}, bf16[8,16,512]{2,1,0:T(8,128)(2,1)S(1)}, u32[]{:S(2)}, u32[]{:S(2)}) collective-permute-start(bf16[8,16,512]{2,1,0:T(8,128)(2,1)S(1)} %copy-done.1), channel_id=1, source_target_pairs={{0,8},{2,10},{4,12},{6,14},{8,0},{10,2},{12,4},{14,6},{1,9},{3,11}... | collective-permute-start | bytes 393224 | tf_op jit(solution)/shard_map/ppermute | solution.py:33
  41.1 2.6 %collective-permute-start.8 = (bf16[8,16,512]{2,1,0:T(8,128)(2,1)S(1)}, bf16[8,16,512]{2,1,0:T(8,128)(2,1)S(1)}, u32[]{:S(2)}, u32[]{:S(2)}) collective-permute-start(bf16[8,16,512]{2,1,0:T(8,128)(2,1)S(1)} %collective-permute-done.3.refs_4_), channel_id=1, source_target_pairs={{0,14},{2,0},{4,2},{6,4},{8,6},{10,8},{12,10},{14,12},{1,15},{3,1}... | collective-permute-start | bytes 393224 | tf_op jit(solution)/shard_map/ppermute | solution.py:33
  47.1 1.9 %collective-permute-done.8.refs_6_ = bf16[8,16,512]{2,1,0:T(8,128)(2,1)S(1)} collective-permute-done((bf16[8,16,512]{2,1,0:T(8,128)(2,1)S(1)}, bf16[8,16,512]{2,1,0:T(8,128)(2,1)S(1)}, u32[]{:S(2)}, u32[]{:S(2)}) %collective-permute-start.8) | collective-permute-done | bytes 131104 | tf_op jit(solution)/shard_map/ppermute | solution.py:33
  49.9 1.7 %collective-permute-done.10 = bf16[24,16,512]{2,1,0:T(8,128)(2,1)S(1)} collective-permute-done((bf16[24,16,512]{2,1,0:T(8,128)(2,1)S(1)}, bf16[24,16,512]{2,1,0:T(8,128)(2,1)S(1)}, u32[]{:S(2)}, u32[]{:S(2)}) %collective-permute-start.10) | collective-permute-done | bytes 393248 | tf_op jit(solution)/shard_map/ppermute | solution.py:29
  51.7 2.3 %collective-permute-start.11 = (bf16[6,16,512]{2,1,0:T(8,128)(2,1)S(1)}, bf16[6,16,512]{2,1,0:T(8,128)(2,1)S(1)}, u32[]{:S(2)}, u32[]{:S(2)}) collective-permute-start(bf16[6,16,512]{2,1,0:T(8,128)(2,1)S(1)} %get-tuple-element.143), channel_id=1, source_target_pairs={{0,192},{64,128},{128,64},{192,0},{1,193},{65,129},{129,65},{193,1... | collective-permute-start | bytes 294920 | tf_op jit(solution)/shard_map/ppermute | solution.py:43
  55.1 1.4 collective-permute-start.13
  57.9 1.8 %collective-permute-done.12 = bf16[6,16,512]{2,1,0:T(8,128)(2,1)S(1)} collective-permute-done((bf16[6,16,512]{2,1,0:T(8,128)(2,1)S(1)}, bf16[6,16,512]{2,1,0:T(8,128)(2,1)S(1)}, u32[]{:S(2)}, u32[]{:S(2)}) %collective-permute-start.12) | collective-permute-done | bytes 98336 | tf_op jit(solution)/shard_map/ppermute | solution.py:43
  59.7 2.1 %collective-permute-done.13 = bf16[6,16,512]{2,1,0:T(8,128)(2,1)S(1)} collective-permute-done((bf16[6,16,512]{2,1,0:T(8,128)(2,1)S(1)}, bf16[6,16,512]{2,1,0:T(8,128)(2,1)S(1)}, u32[]{:S(2)}, u32[]{:S(2)}) %collective-permute-start.13) | collective-permute-done | bytes 98336 | tf_op jit(solution)/shard_map/ppermute | solution.py:43
  62.8 2.8 %collective-permute-start.16 = (bf16[2,6,16,512]{3,2,1,0:T(8,128)(2,1)}, bf16[2,6,16,512]{3,2,1,0:T(8,128)(2,1)}, u32[]{:S(2)}, u32[]{:S(2)}) collective-permute-start(bf16[2,6,16,512]{3,2,1,0:T(8,128)(2,1)} %fusion.1), channel_id=1, source_target_pairs={{0,96},{32,64},{64,32},{96,0},{1,97},{33,65},{65,33},{97,1},{2,98}... | collective-permute-start | bytes 589832 | tf_op jit(solution)/shard_map/ppermute | solution.py:52
  65.6 3.0 %collective-permute-start.15 = (bf16[2,6,16,512]{3,2,1,0:T(8,128)(2,1)}, bf16[2,6,16,512]{3,2,1,0:T(8,128)(2,1)}, u32[]{:S(2)}, u32[]{:S(2)}) collective-permute-start(bf16[2,6,16,512]{3,2,1,0:T(8,128)(2,1)} %fusion.1), channel_id=1, source_target_pairs={{0,64},{32,96},{64,0},{96,32},{1,65},{33,97},{65,1},{97,33},{2,66}... | collective-permute-start | bytes 589832 | tf_op jit(solution)/shard_map/ppermute | solution.py:52
  71.4 2.7 %collective-permute-done.15 = bf16[2,6,16,512]{3,2,1,0:T(8,128)(2,1)} collective-permute-done((bf16[2,6,16,512]{3,2,1,0:T(8,128)(2,1)}, bf16[2,6,16,512]{3,2,1,0:T(8,128)(2,1)}, u32[]{:S(2)}, u32[]{:S(2)}) %collective-permute-start.15) | collective-permute-done | bytes 196640 | tf_op jit(solution)/shard_map/ppermute | solution.py:52
  76.8 4.1 %all-gather.3.cloned.1.call-done = bf16[16,384,512]{2,1,0:T(8,128)(2,1)} async-done(((bf16[1,384,512]{2,1,0:T(8,128)(2,1)}), bf16[16,384,512]{2,1,0:T(8,128)(2,1)}) %all-gather.3.cloned.1.call-update) | async-done | bytes 6291472 | tf_op jit(solution)/shard_map/all_gather | solution.py:37
  80.8 3.2 %kv.8 = (bf16[3,256,512]{2,1,0:T(8,128)(2,1)S(1)}, bf16[3,512,256]{2,1,0:T(8,128)(2,1)S(1)}) custom-call(s32[1]{0:T(128)} %constant.81.clone.1.layer_ref, bf16[4,2,6,16,512]{4,3,2,1,0:T(8,128)(2,1)S(1)} %pad_maximum_fusion.enc_ref, bf16[16,6,2,2,16,512]{5,4,3,2,1,0:T(8,128)(2,1)} %bitcast.56), custom_call_target="tpu_custom_call" | custom-call | flops 805306368 | bytes 4194304 | tf_op jit(solution)/shard_map/kv/pallas_call | solution.py:105
  86.1 1.5 collective-permute-start.18
  88.4 3.2 %kv.9 = (bf16[3,256,512]{2,1,0:T(8,128)(2,1)S(1)}, bf16[3,512,256]{2,1,0:T(8,128)(2,1)S(1)}) custom-call(s32[1]{0:T(128)} %constant.82.clone.1.layer_ref, bf16[4,2,6,16,512]{4,3,2,1,0:T(8,128)(2,1)S(1)} %pad_maximum_fusion.enc_ref, bf16[16,6,2,2,16,512]{5,4,3,2,1,0:T(8,128)(2,1)} %bitcast.57), custom_call_target="tpu_custom_call" | custom-call | flops 805306368 | bytes 4194304 | tf_op jit(solution)/shard_map/kv/pallas_call | solution.py:105
  93.8 1.4 collective-permute-start.21
  96.5 3.2 %kv.10 = (bf16[3,256,512]{2,1,0:T(8,128)(2,1)S(1)}, bf16[3,512,256]{2,1,0:T(8,128)(2,1)S(1)}) custom-call(s32[1]{0:T(128)} %constant.83.clone.1.layer_ref, bf16[4,2,6,16,512]{4,3,2,1,0:T(8,128)(2,1)S(1)} %pad_maximum_fusion.enc_ref, bf16[16,6,2,2,16,512]{5,4,3,2,1,0:T(8,128)(2,1)} %bitcast.58), custom_call_target="tpu_custom_call" | custom-call | flops 805306368 | bytes 4194304 | tf_op jit(solution)/shard_map/kv/pallas_call | solution.py:105
  104.1 3.2 %kv.11 = (bf16[3,256,512]{2,1,0:T(8,128)(2,1)S(1)}, bf16[3,512,256]{2,1,0:T(8,128)(2,1)S(1)}) custom-call(s32[1]{0:T(128)} %constant.84.clone.1.layer_ref, bf16[4,2,6,16,512]{4,3,2,1,0:T(8,128)(2,1)S(1)} %pad_maximum_fusion.enc_ref, bf16[16,6,2,2,16,512]{5,4,3,2,1,0:T(8,128)(2,1)} %bitcast.59), custom_call_target="tpu_custom_call" | custom-call | flops 805306368 | bytes 4194304 | tf_op jit(solution)/shard_map/kv/pallas_call | solution.py:105
  111.7 3.2 %kv.12 = (bf16[3,256,512]{2,1,0:T(8,128)(2,1)S(1)}, bf16[3,512,256]{2,1,0:T(8,128)(2,1)S(1)}) custom-call(s32[1]{0:T(128)} %constant.85.clone.1.layer_ref, bf16[4,2,6,16,512]{4,3,2,1,0:T(8,128)(2,1)S(1)} %pad_maximum_fusion.enc_ref, bf16[16,6,2,2,16,512]{5,4,3,2,1,0:T(8,128)(2,1)} %bitcast.60), custom_call_target="tpu_custom_call" | custom-call | flops 805306368 | bytes 4194304 | tf_op jit(solution)/shard_map/kv/pallas_call | solution.py:105
  116.7 1.4 collective-permute-start.30
  119.4 3.2 %kv.13 = (bf16[3,256,512]{2,1,0:T(8,128)(2,1)S(1)}, bf16[3,512,256]{2,1,0:T(8,128)(2,1)S(1)}) custom-call(s32[1]{0:T(128)} %constant.86.clone.1.layer_ref, bf16[4,2,6,16,512]{4,3,2,1,0:T(8,128)(2,1)S(1)} %pad_maximum_fusion.enc_ref, bf16[16,6,2,2,16,512]{5,4,3,2,1,0:T(8,128)(2,1)} %bitcast.61), custom_call_target="tpu_custom_call" | custom-call | flops 805306368 | bytes 4194304 | tf_op jit(solution)/shard_map/kv/pallas_call | solution.py:105
  127.0 3.2 %kv.14 = (bf16[3,256,512]{2,1,0:T(8,128)(2,1)S(1)}, bf16[3,512,256]{2,1,0:T(8,128)(2,1)S(1)}) custom-call(s32[1]{0:T(128)} %constant.81.clone.1.layer_ref, bf16[4,2,6,16,512]{4,3,2,1,0:T(8,128)(2,1)S(1)} %pad_maximum_fusion.enc_ref, bf16[16,2,2,2,16,512]{5,4,3,2,1,0:T(8,128)(2,1)} %bitcast.74), custom_call_target="tpu_custom_call" | custom-call | flops 805306368 | bytes 4194304 | tf_op jit(solution)/shard_map/kv/pallas_call | solution.py:105
  134.6 3.2 %kv.15 = (bf16[3,256,512]{2,1,0:T(8,128)(2,1)S(1)}, bf16[3,512,256]{2,1,0:T(8,128)(2,1)S(1)}) custom-call(s32[1]{0:T(128)} %constant.82.clone.1.layer_ref, bf16[4,2,6,16,512]{4,3,2,1,0:T(8,128)(2,1)S(1)} %pad_maximum_fusion.enc_ref, bf16[16,2,2,2,16,512]{5,4,3,2,1,0:T(8,128)(2,1)} %bitcast.75), custom_call_target="tpu_custom_call" | custom-call | flops 805306368 | bytes 4194304 | tf_op jit(solution)/shard_map/kv/pallas_call | solution.py:105
  139.1 2.4 %collective-permute-start.38 = (bf16[144,256]{1,0:T(8,128)(2,1)S(1)}, bf16[144,256]{1,0:T(8,128)(2,1)S(1)}, u32[]{:S(2)}, u32[]{:S(2)}) collective-permute-start(bf16[144,256]{1,0:T(8,128)(2,1)S(1)} %bitcast.68), channel_id=1, source_target_pairs={{0,192},{64,128},{128,64},{192,0},{1,193},{65,129},{129,65},{193,1... | collective-permute-start | bytes 221192 | tf_op jit(solution)/shard_map/ppermute | solution.py:43
  141.4 3.3 %collective-permute-done.38 = bf16[144,256]{1,0:T(8,128)(2,1)S(1)} collective-permute-done((bf16[144,256]{1,0:T(8,128)(2,1)S(1)}, bf16[144,256]{1,0:T(8,128)(2,1)S(1)}, u32[]{:S(2)}, u32[]{:S(2)}) %collective-permute-start.38) | collective-permute-done | bytes 73760 | tf_op jit(solution)/shard_map/ppermute | solution.py:43
  (129 shorter events, 49.7 us)
Async XLA Ops:
  8.2 16.7 %all-to-all-start = ((bf16[8,2,16,512]{3,2,1,0:T(8,128)(2,1)}), bf16[8,2,16,512]{3,2,1,0:T(8,128)(2,1)S(1)}, u32[]{:S(2)}, u32[]{:S(2)}) async-start(bf16[8,2,16,512]{3,2,1,0:T(8,128)(2,1)} %parts.1), calls=%async_computation | async-start | bytes 524288 | tf_op jit(solution)/shard_map/all_to_all | solution.py:290
  13.3 67.5 %all-gather.3.cloned.1.call-start = ((), (), s32[]{:S(2)}) async-start(), calls=%async_computation.1 | async-start | bytes 6684672 | tf_op jit(solution)/shard_map/all_gather | solution.py:37
  15.6 9.3 %collective-permute-start = (bf16[8,16,512]{2,1,0:T(8,128)(2,1)}, bf16[8,16,512]{2,1,0:T(8,128)(2,1)S(1)}, u32[]{:S(2)}, u32[]{:S(2)}) collective-permute-start(bf16[8,16,512]{2,1,0:T(8,128)(2,1)} %refs_0_), channel_id=1, source_target_pairs={{0,2},{2,4},{4,6},{6,8},{8,10},{10,12},{12,14},{14,0},{1,3},{3,5},... | collective-permute-start | bytes 393224 | tf_op jit(solution)/shard_map/ppermute | solution.py:33
  17.5 7.4 %collective-permute-start.1 = (bf16[8,16,512]{2,1,0:T(8,128)(2,1)}, bf16[8,16,512]{2,1,0:T(8,128)(2,1)S(1)}, u32[]{:S(2)}, u32[]{:S(2)}) collective-permute-start(bf16[8,16,512]{2,1,0:T(8,128)(2,1)} %refs_0_), channel_id=1, source_target_pairs={{0,14},{2,0},{4,2},{6,4},{8,6},{10,8},{12,10},{14,12},{1,15},{3,1}... | collective-permute-start | bytes 393224 | tf_op jit(solution)/shard_map/ppermute | solution.py:33
  24.9 8.7 %collective-permute-start.5 = (bf16[8,2,16,512]{3,2,1,0:T(8,128)(2,1)S(1)}, bf16[8,2,16,512]{3,2,1,0:T(8,128)(2,1)S(1)}, u32[]{:S(2)}, u32[]{:S(2)}) collective-permute-start(bf16[8,2,16,512]{3,2,1,0:T(8,128)(2,1)S(1)} %all-to-all-done), channel_id=1, source_target_pairs={{0,16},{16,0},{1,17},{17,1},{2,18},{18,2},{3,19},{19,3},{4,20},{20... | collective-permute-start | bytes 786440 | tf_op jit(solution)/shard_map/ppermute | solution.py:29
  25.7 8.0 %collective-permute-start.2 = (bf16[8,16,512]{2,1,0:T(8,128)(2,1)S(1)}, bf16[8,16,512]{2,1,0:T(8,128)(2,1)S(1)}, u32[]{:S(2)}, u32[]{:S(2)}) collective-permute-start(bf16[8,16,512]{2,1,0:T(8,128)(2,1)S(1)} %collective-permute-done.refs_1_), channel_id=1, source_target_pairs={{0,2},{2,4},{4,6},{6,8},{8,10},{10,12},{12,14},{14,0},{1,3},{3,5},... | collective-permute-start | bytes 393224 | tf_op jit(solution)/shard_map/ppermute | solution.py:33
  25.7 8.0 %collective-permute-start.3 = (bf16[8,16,512]{2,1,0:T(8,128)(2,1)S(1)}, bf16[8,16,512]{2,1,0:T(8,128)(2,1)S(1)}, u32[]{:S(2)}, u32[]{:S(2)}) collective-permute-start(bf16[8,16,512]{2,1,0:T(8,128)(2,1)S(1)} %collective-permute-done.1.refs_2_), channel_id=1, source_target_pairs={{0,14},{2,0},{4,2},{6,4},{8,6},{10,8},{12,10},{14,12},{1,15},{3,1}... | collective-permute-start | bytes 393224 | tf_op jit(solution)/shard_map/ppermute | solution.py:33
  34.6 92.4 %all-gather.5.cloned.1.call-start = ((), (), s32[]{:S(2)}) async-start(), calls=%async_computation.2 | async-start | bytes 2228224 | tf_op jit(solution)/shard_map/all_gather | solution.py:37
  35.3 10.5 %collective-permute-start.9 = (bf16[8,16,512]{2,1,0:T(8,128)(2,1)S(1)}, bf16[8,16,512]{2,1,0:T(8,128)(2,1)S(1)}, u32[]{:S(2)}, u32[]{:S(2)}) collective-permute-start(bf16[8,16,512]{2,1,0:T(8,128)(2,1)S(1)} %copy-done.1), channel_id=1, source_target_pairs={{0,8},{2,10},{4,12},{6,14},{8,0},{10,2},{12,4},{14,6},{1,9},{3,11}... | collective-permute-start | bytes 393224 | tf_op jit(solution)/shard_map/ppermute | solution.py:33
  39.5 7.7 %collective-permute-start.7 = (bf16[8,16,512]{2,1,0:T(8,128)(2,1)S(1)}, bf16[8,16,512]{2,1,0:T(8,128)(2,1)S(1)}, u32[]{:S(2)}, u32[]{:S(2)}) collective-permute-start(bf16[8,16,512]{2,1,0:T(8,128)(2,1)S(1)} %collective-permute-done.2.refs_3_), channel_id=1, source_target_pairs={{0,2},{2,4},{4,6},{6,8},{8,10},{10,12},{12,14},{14,0},{1,3},{3,5},... | collective-permute-start | bytes 393224 | tf_op jit(solution)/shard_map/ppermute | solution.py:33
  41.1 7.9 %collective-permute-start.8 = (bf16[8,16,512]{2,1,0:T(8,128)(2,1)S(1)}, bf16[8,16,512]{2,1,0:T(8,128)(2,1)S(1)}, u32[]{:S(2)}, u32[]{:S(2)}) collective-permute-start(bf16[8,16,512]{2,1,0:T(8,128)(2,1)S(1)} %collective-permute-done.3.refs_4_), channel_id=1, source_target_pairs={{0,14},{2,0},{4,2},{6,4},{8,6},{10,8},{12,10},{14,12},{1,15},{3,1}... | collective-permute-start | bytes 393224 | tf_op jit(solution)/shard_map/ppermute | solution.py:33
  51.7 6.1 %collective-permute-start.11 = (bf16[6,16,512]{2,1,0:T(8,128)(2,1)S(1)}, bf16[6,16,512]{2,1,0:T(8,128)(2,1)S(1)}, u32[]{:S(2)}, u32[]{:S(2)}) collective-permute-start(bf16[6,16,512]{2,1,0:T(8,128)(2,1)S(1)} %get-tuple-element.143), channel_id=1, source_target_pairs={{0,192},{64,128},{128,64},{192,0},{1,193},{65,129},{129,65},{193,1... | collective-permute-start | bytes 294920 | tf_op jit(solution)/shard_map/ppermute | solution.py:43
  54.1 5.6 %collective-permute-start.12 = (bf16[6,16,512]{2,1,0:T(8,128)(2,1)S(1)}, bf16[6,16,512]{2,1,0:T(8,128)(2,1)S(1)}, u32[]{:S(2)}, u32[]{:S(2)}) collective-permute-start(bf16[6,16,512]{2,1,0:T(8,128)(2,1)S(1)} %get-tuple-element.142), channel_id=1, source_target_pairs={{0,48},{16,32},{32,16},{48,0},{1,49},{17,33},{33,17},{49,1},{2,50}... | collective-permute-start | bytes 294920 | tf_op jit(solution)/shard_map/ppermute | solution.py:43
  55.1 6.7 %collective-permute-start.13 = (bf16[6,16,512]{2,1,0:T(8,128)(2,1)S(1)}, bf16[6,16,512]{2,1,0:T(8,128)(2,1)S(1)}, u32[]{:S(2)}, u32[]{:S(2)}) collective-permute-start(bf16[6,16,512]{2,1,0:T(8,128)(2,1)S(1)} %get-tuple-element.141), channel_id=1, source_target_pairs={{0,240},{16,224},{32,208},{48,192},{64,176},{80,160},{96,144},{112... | collective-permute-start | bytes 294920 | tf_op jit(solution)/shard_map/ppermute | solution.py:43
  62.8 8.6 %collective-permute-start.16 = (bf16[2,6,16,512]{3,2,1,0:T(8,128)(2,1)}, bf16[2,6,16,512]{3,2,1,0:T(8,128)(2,1)}, u32[]{:S(2)}, u32[]{:S(2)}) collective-permute-start(bf16[2,6,16,512]{3,2,1,0:T(8,128)(2,1)} %fusion.1), channel_id=1, source_target_pairs={{0,96},{32,64},{64,32},{96,0},{1,97},{33,65},{65,33},{97,1},{2,98}... | collective-permute-start | bytes 589832 | tf_op jit(solution)/shard_map/ppermute | solution.py:52
  65.6 8.5 %collective-permute-start.15 = (bf16[2,6,16,512]{3,2,1,0:T(8,128)(2,1)}, bf16[2,6,16,512]{3,2,1,0:T(8,128)(2,1)}, u32[]{:S(2)}, u32[]{:S(2)}) collective-permute-start(bf16[2,6,16,512]{3,2,1,0:T(8,128)(2,1)} %fusion.1), channel_id=1, source_target_pairs={{0,64},{32,96},{64,0},{96,32},{1,65},{33,97},{65,1},{97,33},{2,66}... | collective-permute-start | bytes 589832 | tf_op jit(solution)/shard_map/ppermute | solution.py:52
  68.6 6.7 %collective-permute-start.14 = (bf16[2,6,16,512]{3,2,1,0:T(8,128)(2,1)}, bf16[2,6,16,512]{3,2,1,0:T(8,128)(2,1)}, u32[]{:S(2)}, u32[]{:S(2)}) collective-permute-start(bf16[2,6,16,512]{3,2,1,0:T(8,128)(2,1)} %fusion.1), channel_id=1, source_target_pairs={{0,32},{32,0},{64,96},{96,64},{1,33},{33,1},{65,97},{97,65},{2,34}... | collective-permute-start | bytes 589832 | tf_op jit(solution)/shard_map/ppermute | solution.py:52
  84.9 6.8 %collective-permute-start.17 = (f32[2,128]{1,0:T(2,128)S(1)}, f32[2,128]{1,0:T(2,128)S(1)}, u32[]{:S(2)}, u32[]{:S(2)}) collective-permute-start(f32[2,128]{1,0:T(2,128)S(1)} %get-tuple-element.100.s0_ref), channel_id=1, source_target_pairs={{0,32},{32,0},{64,96},{96,64},{1,33},{33,1},{65,97},{97,65},{2,34}... | collective-permute-start | bytes 3080 | tf_op jit(solution)/shard_map/ppermute | solution.py:52
  86.1 5.5 %collective-permute-start.18 = (f32[2,128]{1,0:T(2,128)S(1)}, f32[2,128]{1,0:T(2,128)S(1)}, u32[]{:S(2)}, u32[]{:S(2)}) collective-permute-start(f32[2,128]{1,0:T(2,128)S(1)} %get-tuple-element.100.s0_ref), channel_id=1, source_target_pairs={{0,64},{32,96},{64,0},{96,32},{1,65},{33,97},{65,1},{97,33},{2,66}... | collective-permute-start | bytes 3080 | tf_op jit(solution)/shard_map/ppermute | solution.py:52
  92.9 6.8 %collective-permute-start.20 = (f32[2,128]{1,0:T(2,128)S(1)}, f32[2,128]{1,0:T(2,128)S(1)}, u32[]{:S(2)}, u32[]{:S(2)}) collective-permute-start(f32[2,128]{1,0:T(2,128)S(1)} %get-tuple-element.105.s0_ref), channel_id=1, source_target_pairs={{0,32},{32,0},{64,96},{96,64},{1,33},{33,1},{65,97},{97,65},{2,34}... | collective-permute-start | bytes 3080 | tf_op jit(solution)/shard_map/ppermute | solution.py:52
  93.8 5.8 %collective-permute-start.21 = (f32[2,128]{1,0:T(2,128)S(1)}, f32[2,128]{1,0:T(2,128)S(1)}, u32[]{:S(2)}, u32[]{:S(2)}) collective-permute-start(f32[2,128]{1,0:T(2,128)S(1)} %get-tuple-element.105.s0_ref), channel_id=1, source_target_pairs={{0,64},{32,96},{64,0},{96,32},{1,65},{33,97},{65,1},{97,33},{2,66}... | collective-permute-start | bytes 3080 | tf_op jit(solution)/shard_map/ppermute | solution.py:52
  100.5 6.8 %collective-permute-start.23 = (f32[2,128]{1,0:T(2,128)S(1)}, f32[2,128]{1,0:T(2,128)S(1)}, u32[]{:S(2)}, u32[]{:S(2)}) collective-permute-start(f32[2,128]{1,0:T(2,128)S(1)} %get-tuple-element.110.s0_ref), channel_id=1, source_target_pairs={{0,32},{32,0},{64,96},{96,64},{1,33},{33,1},{65,97},{97,65},{2,34}... | collective-permute-start | bytes 3080 | tf_op jit(solution)/shard_map/ppermute | solution.py:52
  101.5 5.8 %collective-permute-start.24 = (f32[2,128]{1,0:T(2,128)S(1)}, f32[2,128]{1,0:T(2,128)S(1)}, u32[]{:S(2)}, u32[]{:S(2)}) collective-permute-start(f32[2,128]{1,0:T(2,128)S(1)} %get-tuple-element.110.s0_ref), channel_id=1, source_target_pairs={{0,64},{32,96},{64,0},{96,32},{1,65},{33,97},{65,1},{97,33},{2,66}... | collective-permute-start | bytes 3080 | tf_op jit(solution)/shard_map/ppermute | solution.py:52
  108.2 6.8 %collective-permute-start.26 = (f32[2,128]{1,0:T(2,128)S(1)}, f32[2,128]{1,0:T(2,128)S(1)}, u32[]{:S(2)}, u32[]{:S(2)}) collective-permute-start(f32[2,128]{1,0:T(2,128)S(1)} %get-tuple-element.115.s0_ref), channel_id=1, source_target_pairs={{0,32},{32,0},{64,96},{96,64},{1,33},{33,1},{65,97},{97,65},{2,34}... | collective-permute-start | bytes 3080 | tf_op jit(solution)/shard_map/ppermute | solution.py:52
  109.1 5.8 %collective-permute-start.27 = (f32[2,128]{1,0:T(2,128)S(1)}, f32[2,128]{1,0:T(2,128)S(1)}, u32[]{:S(2)}, u32[]{:S(2)}) collective-permute-start(f32[2,128]{1,0:T(2,128)S(1)} %get-tuple-element.115.s0_ref), channel_id=1, source_target_pairs={{0,64},{32,96},{64,0},{96,32},{1,65},{33,97},{65,1},{97,33},{2,66}... | collective-permute-start | bytes 3080 | tf_op jit(solution)/shard_map/ppermute | solution.py:52
  115.8 6.8 %collective-permute-start.29 = (f32[2,128]{1,0:T(2,128)S(1)}, f32[2,128]{1,0:T(2,128)S(1)}, u32[]{:S(2)}, u32[]{:S(2)}) collective-permute-start(f32[2,128]{1,0:T(2,128)S(1)} %get-tuple-element.120.s0_ref), channel_id=1, source_target_pairs={{0,32},{32,0},{64,96},{96,64},{1,33},{33,1},{65,97},{97,65},{2,34}... | collective-permute-start | bytes 3080 | tf_op jit(solution)/shard_map/ppermute | solution.py:52
  116.7 5.8 %collective-permute-start.30 = (f32[2,128]{1,0:T(2,128)S(1)}, f32[2,128]{1,0:T(2,128)S(1)}, u32[]{:S(2)}, u32[]{:S(2)}) collective-permute-start(f32[2,128]{1,0:T(2,128)S(1)} %get-tuple-element.120.s0_ref), channel_id=1, source_target_pairs={{0,64},{32,96},{64,0},{96,32},{1,65},{33,97},{65,1},{97,33},{2,66}... | collective-permute-start | bytes 3080 | tf_op jit(solution)/shard_map/ppermute | solution.py:52
  123.4 6.8 %collective-permute-start.32 = (f32[2,128]{1,0:T(2,128)S(1)}, f32[2,128]{1,0:T(2,128)S(1)}, u32[]{:S(2)}, u32[]{:S(2)}) collective-permute-start(f32[2,128]{1,0:T(2,128)S(1)} %get-tuple-element.125.s0_ref), channel_id=1, source_target_pairs={{0,32},{32,0},{64,96},{96,64},{1,33},{33,1},{65,97},{97,65},{2,34}... | collective-permute-start | bytes 3080 | tf_op jit(solution)/shard_map/ppermute | solution.py:52
  124.3 5.8 %collective-permute-start.33 = (f32[2,128]{1,0:T(2,128)S(1)}, f32[2,128]{1,0:T(2,128)S(1)}, u32[]{:S(2)}, u32[]{:S(2)}) collective-permute-start(f32[2,128]{1,0:T(2,128)S(1)} %get-tuple-element.125.s0_ref), channel_id=1, source_target_pairs={{0,64},{32,96},{64,0},{96,32},{1,65},{33,97},{65,1},{97,33},{2,66}... | collective-permute-start | bytes 3080 | tf_op jit(solution)/shard_map/ppermute | solution.py:52
  131.0 6.8 %collective-permute-start.35 = (f32[2,128]{1,0:T(2,128)S(1)}, f32[2,128]{1,0:T(2,128)S(1)}, u32[]{:S(2)}, u32[]{:S(2)}) collective-permute-start(f32[2,128]{1,0:T(2,128)S(1)} %get-tuple-element.130.s0_ref), channel_id=1, source_target_pairs={{0,32},{32,0},{64,96},{96,64},{1,33},{33,1},{65,97},{97,65},{2,34}... | collective-permute-start | bytes 3080 | tf_op jit(solution)/shard_map/ppermute | solution.py:52
  131.9 5.9 %collective-permute-start.36 = (f32[2,128]{1,0:T(2,128)S(1)}, f32[2,128]{1,0:T(2,128)S(1)}, u32[]{:S(2)}, u32[]{:S(2)}) collective-permute-start(f32[2,128]{1,0:T(2,128)S(1)} %get-tuple-element.130.s0_ref), channel_id=1, source_target_pairs={{0,64},{32,96},{64,0},{96,32},{1,65},{33,97},{65,1},{97,33},{2,66}... | collective-permute-start | bytes 3080 | tf_op jit(solution)/shard_map/ppermute | solution.py:52
  139.1 5.7 %collective-permute-start.38 = (bf16[144,256]{1,0:T(8,128)(2,1)S(1)}, bf16[144,256]{1,0:T(8,128)(2,1)S(1)}, u32[]{:S(2)}, u32[]{:S(2)}) collective-permute-start(bf16[144,256]{1,0:T(8,128)(2,1)S(1)} %bitcast.68), channel_id=1, source_target_pairs={{0,192},{64,128},{128,64},{192,0},{1,193},{65,129},{129,65},{193,1... | collective-permute-start | bytes 221192 | tf_op jit(solution)/shard_map/ppermute | solution.py:43
  (15 other events, 117.1 us)
Sparse Core Ops, SparseCore 0:
  34.7 46.1 all-gather.2
  82.7 38.3 all-gather.4
where the time goes:
time: 153 us; the launch traced here: 152 us
  starting transfers between devices  61.7 us (40%)
  Pallas kernels  34.5 us (23%)
  waiting for transfers between devices  30.9 us (20%)
  between operations  13.9 us (9%)
  local copies, waits for them, and re-layouts  6.74 us (4%)
  other arithmetic  4.58 us (3%)
    ppermute x24, starting transfers between devices, quad(): lax.ppermute(block, axis, [(i, i ^ d) for i in range(4)])  30.8 us
    pallas_call x8, Pallas kernels, make_kv(): pl.pallas_call(kv_kernel, out_shape=(jax.ShapeDtypeStruct((3, 256, 512),...  25.4 us
    ppermute x7, starting transfers between devices, shifted(): lax.ppermute(block, axis, [(i, (i + distance) % size) for i in range(size)])  16.5 us
    ppermute x5, waiting for transfers between devices, flipped(): return lax.ppermute(block, axes, [(i, last - i) for i in range(last + 1)])  8.54 us
    ppermute x5, starting transfers between devices, flipped(): return lax.ppermute(block, axes, [(i, last - i) for i in range(last + 1)])  8.29 us
    ppermute x7, waiting for transfers between devices, shifted(): lax.ppermute(block, axis, [(i, (i + distance) % size) for i in range(size)])  7.5 us
    pallas_call x8, Pallas kernels, run_layer(): pl.pallas_call(functools.partial(layer_kernel, last=last), out_shape=out_...  6.68 us
    ppermute x3, waiting for transfers between devices, swapped(): return lax.ppermute(block, axis, SWAP)  6.32 us
  transfers between devices with their start and end apart: 42, of which 15 were waited for; matrix products, arithmetic and copies ran while one was open for 6% of the time, Pallas kernels for 20%

commit v1 on v0

--- a/solution.py
+++ b/solution.py
@@ -70,34 +70,25 @@
     ]
     for copy in copies:
         copy.start()
-    for copy in copies[:8]:
+    for copy in copies:
         copy.wait()
 
-    def tokens(g):
-        return enc_ref[:, :, pl.ds(2 * g, 2)].reshape(256, 512)
-
-    def keys(g, carry):
+    def group(g, carry):
+        tokens = enc_ref[:, :, pl.ds(2 * g, 2)].reshape(256, 512)
         made = jnp.dot(
-            tokens(g), held[0].reshape(512, 512), preferred_element_type=jnp.float32
+            tokens, held[0].reshape(512, 512), preferred_element_type=jnp.float32
         )
         key_ref[g] = made.astype(jnp.bfloat16)
-        return carry
-
-    lax.fori_loop(0, 3, keys, 0)
-    for copy in copies[8:]:
-        copy.wait()
-
-    def values(g, carry):
         made = lax.dot_general(
             held[1].reshape(512, 512),
-            tokens(g),
+            tokens,
             (((0,), (1,)), ((), ())),
             preferred_element_type=jnp.float32,
         )
         value_ref[g] = made.astype(jnp.bfloat16)
         return carry
 
-    lax.fori_loop(0, 3, values, 0)
+    lax.fori_loop(0, 3, group, 0)
 
 
 def make_kv(encoded, rows, layer):

time: 153 us -> 151 us (0.987)
  Pallas kernels: 34.5 us -> 30.9 us
  waiting for transfers between devices: 30.9 us -> 33 us
    pallas_call x8, Pallas kernels: 25.4 us -> 21.8 us  [make_kv(): pl.pallas_call(kv_kernel, out_shape=(jax.ShapeDtypeStruct((3, 256, 512),...]
    ppermute x24, waiting for transfers between devices: 4.42 us -> 6.36 us  [quad(): lax.ppermute(block, axis, [(i, i ^ d) for i in range(4)])]
  transfers between devices with their start and end apart: 42 -> 42, of which waited for: 15 -> 18; matrix products, arithmetic and copies ran while one was open for 6% -> 6% of each run, Pallas kernels for 20% -> 18%
where the time goes in v1:
time: 151 us
  starting transfers between devices  61.5 us (41%)
  waiting for transfers between devices  33 us (22%)
  Pallas kernels  30.9 us (20%)
  between operations  13.9 us (9%)
  local copies, waits for them, and re-layouts  6.74 us (4%)
  other arithmetic  4.58 us (3%)
    ppermute x24, starting transfers between devices, quad(): lax.ppermute(block, axis, [(i, i ^ d) for i in range(4)])  30.8 us
    pallas_call x8, Pallas kernels, make_kv(): pl.pallas_call(kv_kernel, out_shape=(jax.ShapeDtypeStruct((3, 256, 512),...  21.8 us
    ppermute x7, starting transfers between devices, shifted(): lax.ppermute(block, axis, [(i, (i + distance) % size) for i in range(size)])  16.5 us
    ppermute x5, waiting for transfers between devices, flipped(): return lax.ppermute(block, axes, [(i, last - i) for i in range(last + 1)])  8.73 us
    ppermute x5, starting transfers between devices, flipped(): return lax.ppermute(block, axes, [(i, last - i) for i in range(last + 1)])  8.1 us
    ppermute x7, waiting for transfers between devices, shifted(): lax.ppermute(block, axis, [(i, (i + distance) % size) for i in range(size)])  7.5 us
    pallas_call x8, Pallas kernels, run_layer(): pl.pallas_call(functools.partial(layer_kernel, last=last), out_shape=out_...  6.65 us
    ppermute x24, waiting for transfers between devices, quad(): lax.ppermute(block, axis, [(i, i ^ d) for i in range(4)])  6.36 us
  transfers between devices with their start and end apart: 42, of which 18 were waited for; matrix products, arithmetic and copies ran while one was open for 6% of the time, Pallas kernels for 18%

profile of v1, /device:TPU:4, one launch (start us, length us, event | category | flops | bytes accessed | tf_op | source)
XLA Modules:
  0.0 150.6 jit_solution(16826313069408218510)
XLA Ops:
  6.5 1.7 %parts.1 = bf16[8,2,16,512]{3,2,1,0:T(8,128)(2,1)} custom-call(bf16[1,16,2048]{2,1,0:T(8,128)(2,1)} %key_ref.1, bf16[1,16,2048]{2,1,0:T(8,128)(2,1)} %value_ref.1, f32[1,2048]{1,0:T(1,128)} %gain_ref.1), custom_call_target="tpu_custom_call" | custom-call | tf_op jit(solution)/shard_map/parts/pallas_call | solution.py:251
  8.2 5.1 %all-to-all-start = ((bf16[8,2,16,512]{3,2,1,0:T(8,128)(2,1)}), bf16[8,2,16,512]{3,2,1,0:T(8,128)(2,1)S(1)}, u32[]{:S(2)}, u32[]{:S(2)}) async-start(bf16[8,2,16,512]{3,2,1,0:T(8,128)(2,1)} %parts.1), calls=%async_computation | async-start | bytes 524288 | tf_op jit(solution)/shard_map/all_to_all | solution.py:281
  15.6 1.9 %collective-permute-start = (bf16[8,16,512]{2,1,0:T(8,128)(2,1)}, bf16[8,16,512]{2,1,0:T(8,128)(2,1)S(1)}, u32[]{:S(2)}, u32[]{:S(2)}) collective-permute-start(bf16[8,16,512]{2,1,0:T(8,128)(2,1)} %refs_0_), channel_id=1, source_target_pairs={{0,2},{2,4},{4,6},{6,8},{8,10},{10,12},{12,14},{14,0},{1,3},{3,5},... | collective-permute-start | bytes 393224 | tf_op jit(solution)/shard_map/ppermute | solution.py:33
  17.5 4.0 %collective-permute-start.1 = (bf16[8,16,512]{2,1,0:T(8,128)(2,1)}, bf16[8,16,512]{2,1,0:T(8,128)(2,1)S(1)}, u32[]{:S(2)}, u32[]{:S(2)}) collective-permute-start(bf16[8,16,512]{2,1,0:T(8,128)(2,1)} %refs_0_), channel_id=1, source_target_pairs={{0,14},{2,0},{4,2},{6,4},{8,6},{10,8},{12,10},{14,12},{1,15},{3,1}... | collective-permute-start | bytes 393224 | tf_op jit(solution)/shard_map/ppermute | solution.py:33
  21.6 3.3 %collective-permute-done.refs_1_ = bf16[8,16,512]{2,1,0:T(8,128)(2,1)S(1)} collective-permute-done((bf16[8,16,512]{2,1,0:T(8,128)(2,1)}, bf16[8,16,512]{2,1,0:T(8,128)(2,1)S(1)}, u32[]{:S(2)}, u32[]{:S(2)}) %collective-permute-start) | collective-permute-done | bytes 131104 | tf_op jit(solution)/shard_map/ppermute | solution.py:33
  25.7 3.2 %collective-permute-start.3 = (bf16[8,16,512]{2,1,0:T(8,128)(2,1)S(1)}, bf16[8,16,512]{2,1,0:T(8,128)(2,1)S(1)}, u32[]{:S(2)}, u32[]{:S(2)}) collective-permute-start(bf16[8,16,512]{2,1,0:T(8,128)(2,1)S(1)} %collective-permute-done.1.refs_2_), channel_id=1, source_target_pairs={{0,14},{2,0},{4,2},{6,4},{8,6},{10,8},{12,10},{14,12},{1,15},{3,1}... | collective-permute-start | bytes 393224 | tf_op jit(solution)/shard_map/ppermute | solution.py:33
  30.1 3.5 %collective-permute-done.5 = bf16[8,2,16,512]{3,2,1,0:T(8,128)(2,1)S(1)} collective-permute-done((bf16[8,2,16,512]{3,2,1,0:T(8,128)(2,1)S(1)}, bf16[8,2,16,512]{3,2,1,0:T(8,128)(2,1)S(1)}, u32[]{:S(2)}, u32[]{:S(2)}) %collective-permute-start.5) | collective-permute-done | bytes 262176 | tf_op jit(solution)/shard_map/ppermute | solution.py:29
  35.3 4.1 %collective-permute-start.9 = (bf16[8,16,512]{2,1,0:T(8,128)(2,1)S(1)}, bf16[8,16,512]{2,1,0:T(8,128)(2,1)S(1)}, u32[]{:S(2)}, u32[]{:S(2)}) collective-permute-start(bf16[8,16,512]{2,1,0:T(8,128)(2,1)S(1)} %copy-done.1), channel_id=1, source_target_pairs={{0,8},{2,10},{4,12},{6,14},{8,0},{10,2},{12,4},{14,6},{1,9},{3,11}... | collective-permute-start | bytes 393224 | tf_op jit(solution)/shard_map/ppermute | solution.py:33
  41.1 2.6 %collective-permute-start.8 = (bf16[8,16,512]{2,1,0:T(8,128)(2,1)S(1)}, bf16[8,16,512]{2,1,0:T(8,128)(2,1)S(1)}, u32[]{:S(2)}, u32[]{:S(2)}) collective-permute-start(bf16[8,16,512]{2,1,0:T(8,128)(2,1)S(1)} %collective-permute-done.3.refs_4_), channel_id=1, source_target_pairs={{0,14},{2,0},{4,2},{6,4},{8,6},{10,8},{12,10},{14,12},{1,15},{3,1}... | collective-permute-start | bytes 393224 | tf_op jit(solution)/shard_map/ppermute | solution.py:33
  47.1 1.9 %collective-permute-done.8.refs_6_ = bf16[8,16,512]{2,1,0:T(8,128)(2,1)S(1)} collective-permute-done((bf16[8,16,512]{2,1,0:T(8,128)(2,1)S(1)}, bf16[8,16,512]{2,1,0:T(8,128)(2,1)S(1)}, u32[]{:S(2)}, u32[]{:S(2)}) %collective-permute-start.8) | collective-permute-done | bytes 131104 | tf_op jit(solution)/shard_map/ppermute | solution.py:33
  49.9 1.7 %collective-permute-done.10 = bf16[24,16,512]{2,1,0:T(8,128)(2,1)S(1)} collective-permute-done((bf16[24,16,512]{2,1,0:T(8,128)(2,1)S(1)}, bf16[24,16,512]{2,1,0:T(8,128)(2,1)S(1)}, u32[]{:S(2)}, u32[]{:S(2)}) %collective-permute-start.10) | collective-permute-done | bytes 393248 | tf_op jit(solution)/shard_map/ppermute | solution.py:29
  51.7 2.3 %collective-permute-start.11 = (bf16[6,16,512]{2,1,0:T(8,128)(2,1)S(1)}, bf16[6,16,512]{2,1,0:T(8,128)(2,1)S(1)}, u32[]{:S(2)}, u32[]{:S(2)}) collective-permute-start(bf16[6,16,512]{2,1,0:T(8,128)(2,1)S(1)} %get-tuple-element.143), channel_id=1, source_target_pairs={{0,192},{64,128},{128,64},{192,0},{1,193},{65,129},{129,65},{193,1... | collective-permute-start | bytes 294920 | tf_op jit(solution)/shard_map/ppermute | solution.py:43
  57.9 1.8 %collective-permute-done.12 = bf16[6,16,512]{2,1,0:T(8,128)(2,1)S(1)} collective-permute-done((bf16[6,16,512]{2,1,0:T(8,128)(2,1)S(1)}, bf16[6,16,512]{2,1,0:T(8,128)(2,1)S(1)}, u32[]{:S(2)}, u32[]{:S(2)}) %collective-permute-start.12) | collective-permute-done | bytes 98336 | tf_op jit(solution)/shard_map/ppermute | solution.py:43
  59.7 2.1 %collective-permute-done.13 = bf16[6,16,512]{2,1,0:T(8,128)(2,1)S(1)} collective-permute-done((bf16[6,16,512]{2,1,0:T(8,128)(2,1)S(1)}, bf16[6,16,512]{2,1,0:T(8,128)(2,1)S(1)}, u32[]{:S(2)}, u32[]{:S(2)}) %collective-permute-start.13) | collective-permute-done | bytes 98336 | tf_op jit(solution)/shard_map/ppermute | solution.py:43
  62.8 2.8 %collective-permute-start.16 = (bf16[2,6,16,512]{3,2,1,0:T(8,128)(2,1)}, bf16[2,6,16,512]{3,2,1,0:T(8,128)(2,1)}, u32[]{:S(2)}, u32[]{:S(2)}) collective-permute-start(bf16[2,6,16,512]{3,2,1,0:T(8,128)(2,1)} %fusion.1), channel_id=1, source_target_pairs={{0,96},{32,64},{64,32},{96,0},{1,97},{33,65},{65,33},{97,1},{2,98}... | collective-permute-start | bytes 589832 | tf_op jit(solution)/shard_map/ppermute | solution.py:52
  65.6 3.0 %collective-permute-start.15 = (bf16[2,6,16,512]{3,2,1,0:T(8,128)(2,1)}, bf16[2,6,16,512]{3,2,1,0:T(8,128)(2,1)}, u32[]{:S(2)}, u32[]{:S(2)}) collective-permute-start(bf16[2,6,16,512]{3,2,1,0:T(8,128)(2,1)} %fusion.1), channel_id=1, source_target_pairs={{0,64},{32,96},{64,0},{96,32},{1,65},{33,97},{65,1},{97,33},{2,66}... | collective-permute-start | bytes 589832 | tf_op jit(solution)/shard_map/ppermute | solution.py:52
  71.4 2.7 %collective-permute-done.15 = bf16[2,6,16,512]{3,2,1,0:T(8,128)(2,1)} collective-permute-done((bf16[2,6,16,512]{3,2,1,0:T(8,128)(2,1)}, bf16[2,6,16,512]{3,2,1,0:T(8,128)(2,1)}, u32[]{:S(2)}, u32[]{:S(2)}) %collective-permute-start.15) | collective-permute-done | bytes 196640 | tf_op jit(solution)/shard_map/ppermute | solution.py:52
  76.8 4.1 %all-gather.3.cloned.1.call-done = bf16[16,384,512]{2,1,0:T(8,128)(2,1)} async-done(((bf16[1,384,512]{2,1,0:T(8,128)(2,1)}), bf16[16,384,512]{2,1,0:T(8,128)(2,1)}) %all-gather.3.cloned.1.call-update) | async-done | bytes 6291472 | tf_op jit(solution)/shard_map/all_gather | solution.py:37
  80.8 2.7 %kv.8 = (bf16[3,256,512]{2,1,0:T(8,128)(2,1)S(1)}, bf16[3,512,256]{2,1,0:T(8,128)(2,1)S(1)}) custom-call(s32[1]{0:T(128)} %constant.81.clone.1.layer_ref, bf16[4,2,6,16,512]{4,3,2,1,0:T(8,128)(2,1)S(1)} %pad_maximum_fusion.enc_ref, bf16[16,6,2,2,16,512]{5,4,3,2,1,0:T(8,128)(2,1)} %bitcast.56), custom_call_target="tpu_custom_call" | custom-call | flops 805306368 | bytes 4194304 | tf_op jit(solution)/shard_map/kv/pallas_call | solution.py:96
  85.7 1.5 collective-permute-start.18
  88.0 2.7 %kv.9 = (bf16[3,256,512]{2,1,0:T(8,128)(2,1)S(1)}, bf16[3,512,256]{2,1,0:T(8,128)(2,1)S(1)}) custom-call(s32[1]{0:T(128)} %constant.82.clone.1.layer_ref, bf16[4,2,6,16,512]{4,3,2,1,0:T(8,128)(2,1)S(1)} %pad_maximum_fusion.enc_ref, bf16[16,6,2,2,16,512]{5,4,3,2,1,0:T(8,128)(2,1)} %bitcast.57), custom_call_target="tpu_custom_call" | custom-call | flops 805306368 | bytes 4194304 | tf_op jit(solution)/shard_map/kv/pallas_call | solution.py:96
  94.3 1.7 %collective-permute-start.22 = (f32[2,128]{1,0:T(2,128)S(1)}, f32[2,128]{1,0:T(2,128)S(1)}, u32[]{:S(2)}, u32[]{:S(2)}) collective-permute-start(f32[2,128]{1,0:T(2,128)S(1)} %get-tuple-element.105.s0_ref), channel_id=1, source_target_pairs={{0,96},{32,64},{64,32},{96,0},{1,97},{33,65},{65,33},{97,1},{2,98}... | collective-permute-start | bytes 3080 | tf_op jit(solution)/shard_map/ppermute | solution.py:52
  96.0 2.7 %kv.10 = (bf16[3,256,512]{2,1,0:T(8,128)(2,1)S(1)}, bf16[3,512,256]{2,1,0:T(8,128)(2,1)S(1)}) custom-call(s32[1]{0:T(128)} %constant.83.clone.1.layer_ref, bf16[4,2,6,16,512]{4,3,2,1,0:T(8,128)(2,1)S(1)} %pad_maximum_fusion.enc_ref, bf16[16,6,2,2,16,512]{5,4,3,2,1,0:T(8,128)(2,1)} %bitcast.58), custom_call_target="tpu_custom_call" | custom-call | flops 805306368 | bytes 4194304 | tf_op jit(solution)/shard_map/kv/pallas_call | solution.py:96
  103.2 2.7 %kv.11 = (bf16[3,256,512]{2,1,0:T(8,128)(2,1)S(1)}, bf16[3,512,256]{2,1,0:T(8,128)(2,1)S(1)}) custom-call(s32[1]{0:T(128)} %constant.84.clone.1.layer_ref, bf16[4,2,6,16,512]{4,3,2,1,0:T(8,128)(2,1)S(1)} %pad_maximum_fusion.enc_ref, bf16[16,6,2,2,16,512]{5,4,3,2,1,0:T(8,128)(2,1)} %bitcast.59), custom_call_target="tpu_custom_call" | custom-call | flops 805306368 | bytes 4194304 | tf_op jit(solution)/shard_map/kv/pallas_call | solution.py:96
  109.1 1.7 %collective-permute-start.28 = (f32[2,128]{1,0:T(2,128)S(1)}, f32[2,128]{1,0:T(2,128)S(1)}, u32[]{:S(2)}, u32[]{:S(2)}) collective-permute-start(f32[2,128]{1,0:T(2,128)S(1)} %get-tuple-element.115.s0_ref), channel_id=1, source_target_pairs={{0,96},{32,64},{64,32},{96,0},{1,97},{33,65},{65,33},{97,1},{2,98}... | collective-permute-start | bytes 3080 | tf_op jit(solution)/shard_map/ppermute | solution.py:52
  110.8 2.7 %kv.12 = (bf16[3,256,512]{2,1,0:T(8,128)(2,1)S(1)}, bf16[3,512,256]{2,1,0:T(8,128)(2,1)S(1)}) custom-call(s32[1]{0:T(128)} %constant.85.clone.1.layer_ref, bf16[4,2,6,16,512]{4,3,2,1,0:T(8,128)(2,1)S(1)} %pad_maximum_fusion.enc_ref, bf16[16,6,2,2,16,512]{5,4,3,2,1,0:T(8,128)(2,1)} %bitcast.60), custom_call_target="tpu_custom_call" | custom-call | flops 805306368 | bytes 4194304 | tf_op jit(solution)/shard_map/kv/pallas_call | solution.py:96
  118.0 2.7 %kv.13 = (bf16[3,256,512]{2,1,0:T(8,128)(2,1)S(1)}, bf16[3,512,256]{2,1,0:T(8,128)(2,1)S(1)}) custom-call(s32[1]{0:T(128)} %constant.86.clone.1.layer_ref, bf16[4,2,6,16,512]{4,3,2,1,0:T(8,128)(2,1)S(1)} %pad_maximum_fusion.enc_ref, bf16[16,6,2,2,16,512]{5,4,3,2,1,0:T(8,128)(2,1)} %bitcast.61), custom_call_target="tpu_custom_call" | custom-call | flops 805306368 | bytes 4194304 | tf_op jit(solution)/shard_map/kv/pallas_call | solution.py:96
  124.0 1.7 %collective-permute-start.34 = (f32[2,128]{1,0:T(2,128)S(1)}, f32[2,128]{1,0:T(2,128)S(1)}, u32[]{:S(2)}, u32[]{:S(2)}) collective-permute-start(f32[2,128]{1,0:T(2,128)S(1)} %get-tuple-element.125.s0_ref), channel_id=1, source_target_pairs={{0,96},{32,64},{64,32},{96,0},{1,97},{33,65},{65,33},{97,1},{2,98}... | collective-permute-start | bytes 3080 | tf_op jit(solution)/shard_map/ppermute | solution.py:52
  125.7 2.7 %kv.14 = (bf16[3,256,512]{2,1,0:T(8,128)(2,1)S(1)}, bf16[3,512,256]{2,1,0:T(8,128)(2,1)S(1)}) custom-call(s32[1]{0:T(128)} %constant.81.clone.1.layer_ref, bf16[4,2,6,16,512]{4,3,2,1,0:T(8,128)(2,1)S(1)} %pad_maximum_fusion.enc_ref, bf16[16,2,2,2,16,512]{5,4,3,2,1,0:T(8,128)(2,1)} %bitcast.74), custom_call_target="tpu_custom_call" | custom-call | flops 805306368 | bytes 4194304 | tf_op jit(solution)/shard_map/kv/pallas_call | solution.py:96
  132.8 2.7 %kv.15 = (bf16[3,256,512]{2,1,0:T(8,128)(2,1)S(1)}, bf16[3,512,256]{2,1,0:T(8,128)(2,1)S(1)}) custom-call(s32[1]{0:T(128)} %constant.82.clone.1.layer_ref, bf16[4,2,6,16,512]{4,3,2,1,0:T(8,128)(2,1)S(1)} %pad_maximum_fusion.enc_ref, bf16[16,2,2,2,16,512]{5,4,3,2,1,0:T(8,128)(2,1)} %bitcast.75), custom_call_target="tpu_custom_call" | custom-call | flops 805306368 | bytes 4194304 | tf_op jit(solution)/shard_map/kv/pallas_call | solution.py:96
  137.3 2.2 %collective-permute-start.38 = (bf16[144,256]{1,0:T(8,128)(2,1)S(1)}, bf16[144,256]{1,0:T(8,128)(2,1)S(1)}, u32[]{:S(2)}, u32[]{:S(2)}) collective-permute-start(bf16[144,256]{1,0:T(8,128)(2,1)S(1)} %bitcast.68), channel_id=1, source_target_pairs={{0,192},{64,128},{128,64},{192,0},{1,193},{65,129},{129,65},{193,1... | collective-permute-start | bytes 221192 | tf_op jit(solution)/shard_map/ppermute | solution.py:43
  139.5 3.5 %collective-permute-done.38 = bf16[144,256]{1,0:T(8,128)(2,1)S(1)} collective-permute-done((bf16[144,256]{1,0:T(8,128)(2,1)S(1)}, bf16[144,256]{1,0:T(8,128)(2,1)S(1)}, u32[]{:S(2)}, u32[]{:S(2)}) %collective-permute-start.38) | collective-permute-done | bytes 73760 | tf_op jit(solution)/shard_map/ppermute | solution.py:43
  (129 shorter events, 50.7 us)
Async XLA Ops:
  8.2 16.7 %all-to-all-start = ((bf16[8,2,16,512]{3,2,1,0:T(8,128)(2,1)}), bf16[8,2,16,512]{3,2,1,0:T(8,128)(2,1)S(1)}, u32[]{:S(2)}, u32[]{:S(2)}) async-start(bf16[8,2,16,512]{3,2,1,0:T(8,128)(2,1)} %parts.1), calls=%async_computation | async-start | bytes 524288 | tf_op jit(solution)/shard_map/all_to_all | solution.py:281
  13.3 67.5 %all-gather.3.cloned.1.call-start = ((), (), s32[]{:S(2)}) async-start(), calls=%async_computation.1 | async-start | bytes 6684672 | tf_op jit(solution)/shard_map/all_gather | solution.py:37
  15.6 9.3 %collective-permute-start = (bf16[8,16,512]{2,1,0:T(8,128)(2,1)}, bf16[8,16,512]{2,1,0:T(8,128)(2,1)S(1)}, u32[]{:S(2)}, u32[]{:S(2)}) collective-permute-start(bf16[8,16,512]{2,1,0:T(8,128)(2,1)} %refs_0_), channel_id=1, source_target_pairs={{0,2},{2,4},{4,6},{6,8},{8,10},{10,12},{12,14},{14,0},{1,3},{3,5},... | collective-permute-start | bytes 393224 | tf_op jit(solution)/shard_map/ppermute | solution.py:33
  17.5 7.4 %collective-permute-start.1 = (bf16[8,16,512]{2,1,0:T(8,128)(2,1)}, bf16[8,16,512]{2,1,0:T(8,128)(2,1)S(1)}, u32[]{:S(2)}, u32[]{:S(2)}) collective-permute-start(bf16[8,16,512]{2,1,0:T(8,128)(2,1)} %refs_0_), channel_id=1, source_target_pairs={{0,14},{2,0},{4,2},{6,4},{8,6},{10,8},{12,10},{14,12},{1,15},{3,1}... | collective-permute-start | bytes 393224 | tf_op jit(solution)/shard_map/ppermute | solution.py:33
  24.9 8.7 %collective-permute-start.5 = (bf16[8,2,16,512]{3,2,1,0:T(8,128)(2,1)S(1)}, bf16[8,2,16,512]{3,2,1,0:T(8,128)(2,1)S(1)}, u32[]{:S(2)}, u32[]{:S(2)}) collective-permute-start(bf16[8,2,16,512]{3,2,1,0:T(8,128)(2,1)S(1)} %all-to-all-done), channel_id=1, source_target_pairs={{0,16},{16,0},{1,17},{17,1},{2,18},{18,2},{3,19},{19,3},{4,20},{20... | collective-permute-start | bytes 786440 | tf_op jit(solution)/shard_map/ppermute | solution.py:29
  25.7 8.0 %collective-permute-start.2 = (bf16[8,16,512]{2,1,0:T(8,128)(2,1)S(1)}, bf16[8,16,512]{2,1,0:T(8,128)(2,1)S(1)}, u32[]{:S(2)}, u32[]{:S(2)}) collective-permute-start(bf16[8,16,512]{2,1,0:T(8,128)(2,1)S(1)} %collective-permute-done.refs_1_), channel_id=1, source_target_pairs={{0,2},{2,4},{4,6},{6,8},{8,10},{10,12},{12,14},{14,0},{1,3},{3,5},... | collective-permute-start | bytes 393224 | tf_op jit(solution)/shard_map/ppermute | solution.py:33
  25.7 8.0 %collective-permute-start.3 = (bf16[8,16,512]{2,1,0:T(8,128)(2,1)S(1)}, bf16[8,16,512]{2,1,0:T(8,128)(2,1)S(1)}, u32[]{:S(2)}, u32[]{:S(2)}) collective-permute-start(bf16[8,16,512]{2,1,0:T(8,128)(2,1)S(1)} %collective-permute-done.1.refs_2_), channel_id=1, source_target_pairs={{0,14},{2,0},{4,2},{6,4},{8,6},{10,8},{12,10},{14,12},{1,15},{3,1}... | collective-permute-start | bytes 393224 | tf_op jit(solution)/shard_map/ppermute | solution.py:33
  34.6 91.1 %all-gather.5.cloned.1.call-start = ((), (), s32[]{:S(2)}) async-start(), calls=%async_computation.2 | async-start | bytes 2228224 | tf_op jit(solution)/shard_map/all_gather | solution.py:37
  35.3 10.5 %collective-permute-start.9 = (bf16[8,16,512]{2,1,0:T(8,128)(2,1)S(1)}, bf16[8,16,512]{2,1,0:T(8,128)(2,1)S(1)}, u32[]{:S(2)}, u32[]{:S(2)}) collective-permute-start(bf16[8,16,512]{2,1,0:T(8,128)(2,1)S(1)} %copy-done.1), channel_id=1, source_target_pairs={{0,8},{2,10},{4,12},{6,14},{8,0},{10,2},{12,4},{14,6},{1,9},{3,11}... | collective-permute-start | bytes 393224 | tf_op jit(solution)/shard_map/ppermute | solution.py:33
  39.5 7.7 %collective-permute-start.7 = (bf16[8,16,512]{2,1,0:T(8,128)(2,1)S(1)}, bf16[8,16,512]{2,1,0:T(8,128)(2,1)S(1)}, u32[]{:S(2)}, u32[]{:S(2)}) collective-permute-start(bf16[8,16,512]{2,1,0:T(8,128)(2,1)S(1)} %collective-permute-done.2.refs_3_), channel_id=1, source_target_pairs={{0,2},{2,4},{4,6},{6,8},{8,10},{10,12},{12,14},{14,0},{1,3},{3,5},... | collective-permute-start | bytes 393224 | tf_op jit(solution)/shard_map/ppermute | solution.py:33
  41.1 7.9 %collective-permute-start.8 = (bf16[8,16,512]{2,1,0:T(8,128)(2,1)S(1)}, bf16[8,16,512]{2,1,0:T(8,128)(2,1)S(1)}, u32[]{:S(2)}, u32[]{:S(2)}) collective-permute-start(bf16[8,16,512]{2,1,0:T(8,128)(2,1)S(1)} %collective-permute-done.3.refs_4_), channel_id=1, source_target_pairs={{0,14},{2,0},{4,2},{6,4},{8,6},{10,8},{12,10},{14,12},{1,15},{3,1}... | collective-permute-start | bytes 393224 | tf_op jit(solution)/shard_map/ppermute | solution.py:33
  51.7 6.1 %collective-permute-start.11 = (bf16[6,16,512]{2,1,0:T(8,128)(2,1)S(1)}, bf16[6,16,512]{2,1,0:T(8,128)(2,1)S(1)}, u32[]{:S(2)}, u32[]{:S(2)}) collective-permute-start(bf16[6,16,512]{2,1,0:T(8,128)(2,1)S(1)} %get-tuple-element.143), channel_id=1, source_target_pairs={{0,192},{64,128},{128,64},{192,0},{1,193},{65,129},{129,65},{193,1... | collective-permute-start | bytes 294920 | tf_op jit(solution)/shard_map/ppermute | solution.py:43
  54.1 5.6 %collective-permute-start.12 = (bf16[6,16,512]{2,1,0:T(8,128)(2,1)S(1)}, bf16[6,16,512]{2,1,0:T(8,128)(2,1)S(1)}, u32[]{:S(2)}, u32[]{:S(2)}) collective-permute-start(bf16[6,16,512]{2,1,0:T(8,128)(2,1)S(1)} %get-tuple-element.142), channel_id=1, source_target_pairs={{0,48},{16,32},{32,16},{48,0},{1,49},{17,33},{33,17},{49,1},{2,50}... | collective-permute-start | bytes 294920 | tf_op jit(solution)/shard_map/ppermute | solution.py:43
  55.1 6.7 %collective-permute-start.13 = (bf16[6,16,512]{2,1,0:T(8,128)(2,1)S(1)}, bf16[6,16,512]{2,1,0:T(8,128)(2,1)S(1)}, u32[]{:S(2)}, u32[]{:S(2)}) collective-permute-start(bf16[6,16,512]{2,1,0:T(8,128)(2,1)S(1)} %get-tuple-element.141), channel_id=1, source_target_pairs={{0,240},{16,224},{32,208},{48,192},{64,176},{80,160},{96,144},{112... | collective-permute-start | bytes 294920 | tf_op jit(solution)/shard_map/ppermute | solution.py:43
  62.8 8.6 %collective-permute-start.16 = (bf16[2,6,16,512]{3,2,1,0:T(8,128)(2,1)}, bf16[2,6,16,512]{3,2,1,0:T(8,128)(2,1)}, u32[]{:S(2)}, u32[]{:S(2)}) collective-permute-start(bf16[2,6,16,512]{3,2,1,0:T(8,128)(2,1)} %fusion.1), channel_id=1, source_target_pairs={{0,96},{32,64},{64,32},{96,0},{1,97},{33,65},{65,33},{97,1},{2,98}... | collective-permute-start | bytes 589832 | tf_op jit(solution)/shard_map/ppermute | solution.py:52
  65.6 8.5 %collective-permute-start.15 = (bf16[2,6,16,512]{3,2,1,0:T(8,128)(2,1)}, bf16[2,6,16,512]{3,2,1,0:T(8,128)(2,1)}, u32[]{:S(2)}, u32[]{:S(2)}) collective-permute-start(bf16[2,6,16,512]{3,2,1,0:T(8,128)(2,1)} %fusion.1), channel_id=1, source_target_pairs={{0,64},{32,96},{64,0},{96,32},{1,65},{33,97},{65,1},{97,33},{2,66}... | collective-permute-start | bytes 589832 | tf_op jit(solution)/shard_map/ppermute | solution.py:52
  68.6 6.7 %collective-permute-start.14 = (bf16[2,6,16,512]{3,2,1,0:T(8,128)(2,1)}, bf16[2,6,16,512]{3,2,1,0:T(8,128)(2,1)}, u32[]{:S(2)}, u32[]{:S(2)}) collective-permute-start(bf16[2,6,16,512]{3,2,1,0:T(8,128)(2,1)} %fusion.1), channel_id=1, source_target_pairs={{0,32},{32,0},{64,96},{96,64},{1,33},{33,1},{65,97},{97,65},{2,34}... | collective-permute-start | bytes 589832 | tf_op jit(solution)/shard_map/ppermute | solution.py:52
  84.4 6.3 %collective-permute-start.17 = (f32[2,128]{1,0:T(2,128)S(1)}, f32[2,128]{1,0:T(2,128)S(1)}, u32[]{:S(2)}, u32[]{:S(2)}) collective-permute-start(f32[2,128]{1,0:T(2,128)S(1)} %get-tuple-element.100.s0_ref), channel_id=1, source_target_pairs={{0,32},{32,0},{64,96},{96,64},{1,33},{33,1},{65,97},{97,65},{2,34}... | collective-permute-start | bytes 3080 | tf_op jit(solution)/shard_map/ppermute | solution.py:52
  85.7 5.1 %collective-permute-start.18 = (f32[2,128]{1,0:T(2,128)S(1)}, f32[2,128]{1,0:T(2,128)S(1)}, u32[]{:S(2)}, u32[]{:S(2)}) collective-permute-start(f32[2,128]{1,0:T(2,128)S(1)} %get-tuple-element.100.s0_ref), channel_id=1, source_target_pairs={{0,64},{32,96},{64,0},{96,32},{1,65},{33,97},{65,1},{97,33},{2,66}... | collective-permute-start | bytes 3080 | tf_op jit(solution)/shard_map/ppermute | solution.py:52
  92.5 6.3 %collective-permute-start.20 = (f32[2,128]{1,0:T(2,128)S(1)}, f32[2,128]{1,0:T(2,128)S(1)}, u32[]{:S(2)}, u32[]{:S(2)}) collective-permute-start(f32[2,128]{1,0:T(2,128)S(1)} %get-tuple-element.105.s0_ref), channel_id=1, source_target_pairs={{0,32},{32,0},{64,96},{96,64},{1,33},{33,1},{65,97},{97,65},{2,34}... | collective-permute-start | bytes 3080 | tf_op jit(solution)/shard_map/ppermute | solution.py:52
  93.4 5.4 %collective-permute-start.21 = (f32[2,128]{1,0:T(2,128)S(1)}, f32[2,128]{1,0:T(2,128)S(1)}, u32[]{:S(2)}, u32[]{:S(2)}) collective-permute-start(f32[2,128]{1,0:T(2,128)S(1)} %get-tuple-element.105.s0_ref), channel_id=1, source_target_pairs={{0,64},{32,96},{64,0},{96,32},{1,65},{33,97},{65,1},{97,33},{2,66}... | collective-permute-start | bytes 3080 | tf_op jit(solution)/shard_map/ppermute | solution.py:52
  99.6 6.3 %collective-permute-start.23 = (f32[2,128]{1,0:T(2,128)S(1)}, f32[2,128]{1,0:T(2,128)S(1)}, u32[]{:S(2)}, u32[]{:S(2)}) collective-permute-start(f32[2,128]{1,0:T(2,128)S(1)} %get-tuple-element.110.s0_ref), channel_id=1, source_target_pairs={{0,32},{32,0},{64,96},{96,64},{1,33},{33,1},{65,97},{97,65},{2,34}... | collective-permute-start | bytes 3080 | tf_op jit(solution)/shard_map/ppermute | solution.py:52
  100.6 5.4 %collective-permute-start.24 = (f32[2,128]{1,0:T(2,128)S(1)}, f32[2,128]{1,0:T(2,128)S(1)}, u32[]{:S(2)}, u32[]{:S(2)}) collective-permute-start(f32[2,128]{1,0:T(2,128)S(1)} %get-tuple-element.110.s0_ref), channel_id=1, source_target_pairs={{0,64},{32,96},{64,0},{96,32},{1,65},{33,97},{65,1},{97,33},{2,66}... | collective-permute-start | bytes 3080 | tf_op jit(solution)/shard_map/ppermute | solution.py:52
  107.3 6.3 %collective-permute-start.26 = (f32[2,128]{1,0:T(2,128)S(1)}, f32[2,128]{1,0:T(2,128)S(1)}, u32[]{:S(2)}, u32[]{:S(2)}) collective-permute-start(f32[2,128]{1,0:T(2,128)S(1)} %get-tuple-element.115.s0_ref), channel_id=1, source_target_pairs={{0,32},{32,0},{64,96},{96,64},{1,33},{33,1},{65,97},{97,65},{2,34}... | collective-permute-start | bytes 3080 | tf_op jit(solution)/shard_map/ppermute | solution.py:52
  108.2 5.4 %collective-permute-start.27 = (f32[2,128]{1,0:T(2,128)S(1)}, f32[2,128]{1,0:T(2,128)S(1)}, u32[]{:S(2)}, u32[]{:S(2)}) collective-permute-start(f32[2,128]{1,0:T(2,128)S(1)} %get-tuple-element.115.s0_ref), channel_id=1, source_target_pairs={{0,64},{32,96},{64,0},{96,32},{1,65},{33,97},{65,1},{97,33},{2,66}... | collective-permute-start | bytes 3080 | tf_op jit(solution)/shard_map/ppermute | solution.py:52
  114.4 6.3 %collective-permute-start.29 = (f32[2,128]{1,0:T(2,128)S(1)}, f32[2,128]{1,0:T(2,128)S(1)}, u32[]{:S(2)}, u32[]{:S(2)}) collective-permute-start(f32[2,128]{1,0:T(2,128)S(1)} %get-tuple-element.120.s0_ref), channel_id=1, source_target_pairs={{0,32},{32,0},{64,96},{96,64},{1,33},{33,1},{65,97},{97,65},{2,34}... | collective-permute-start | bytes 3080 | tf_op jit(solution)/shard_map/ppermute | solution.py:52
  115.4 5.4 %collective-permute-start.30 = (f32[2,128]{1,0:T(2,128)S(1)}, f32[2,128]{1,0:T(2,128)S(1)}, u32[]{:S(2)}, u32[]{:S(2)}) collective-permute-start(f32[2,128]{1,0:T(2,128)S(1)} %get-tuple-element.120.s0_ref), channel_id=1, source_target_pairs={{0,64},{32,96},{64,0},{96,32},{1,65},{33,97},{65,1},{97,33},{2,66}... | collective-permute-start | bytes 3080 | tf_op jit(solution)/shard_map/ppermute | solution.py:52
  122.1 6.3 %collective-permute-start.32 = (f32[2,128]{1,0:T(2,128)S(1)}, f32[2,128]{1,0:T(2,128)S(1)}, u32[]{:S(2)}, u32[]{:S(2)}) collective-permute-start(f32[2,128]{1,0:T(2,128)S(1)} %get-tuple-element.125.s0_ref), channel_id=1, source_target_pairs={{0,32},{32,0},{64,96},{96,64},{1,33},{33,1},{65,97},{97,65},{2,34}... | collective-permute-start | bytes 3080 | tf_op jit(solution)/shard_map/ppermute | solution.py:52
  123.0 5.4 %collective-permute-start.33 = (f32[2,128]{1,0:T(2,128)S(1)}, f32[2,128]{1,0:T(2,128)S(1)}, u32[]{:S(2)}, u32[]{:S(2)}) collective-permute-start(f32[2,128]{1,0:T(2,128)S(1)} %get-tuple-element.125.s0_ref), channel_id=1, source_target_pairs={{0,64},{32,96},{64,0},{96,32},{1,65},{33,97},{65,1},{97,33},{2,66}... | collective-permute-start | bytes 3080 | tf_op jit(solution)/shard_map/ppermute | solution.py:52
  129.3 6.3 %collective-permute-start.35 = (f32[2,128]{1,0:T(2,128)S(1)}, f32[2,128]{1,0:T(2,128)S(1)}, u32[]{:S(2)}, u32[]{:S(2)}) collective-permute-start(f32[2,128]{1,0:T(2,128)S(1)} %get-tuple-element.130.s0_ref), channel_id=1, source_target_pairs={{0,32},{32,0},{64,96},{96,64},{1,33},{33,1},{65,97},{97,65},{2,34}... | collective-permute-start | bytes 3080 | tf_op jit(solution)/shard_map/ppermute | solution.py:52
  130.2 5.4 %collective-permute-start.36 = (f32[2,128]{1,0:T(2,128)S(1)}, f32[2,128]{1,0:T(2,128)S(1)}, u32[]{:S(2)}, u32[]{:S(2)}) collective-permute-start(f32[2,128]{1,0:T(2,128)S(1)} %get-tuple-element.130.s0_ref), channel_id=1, source_target_pairs={{0,64},{32,96},{64,0},{96,32},{1,65},{33,97},{65,1},{97,33},{2,66}... | collective-permute-start | bytes 3080 | tf_op jit(solution)/shard_map/ppermute | solution.py:52
  137.3 5.7 %collective-permute-start.38 = (bf16[144,256]{1,0:T(8,128)(2,1)S(1)}, bf16[144,256]{1,0:T(8,128)(2,1)S(1)}, u32[]{:S(2)}, u32[]{:S(2)}) collective-permute-start(bf16[144,256]{1,0:T(8,128)(2,1)S(1)} %bitcast.68), channel_id=1, source_target_pairs={{0,192},{64,128},{128,64},{192,0},{1,193},{65,129},{129,65},{193,1... | collective-permute-start | bytes 221192 | tf_op jit(solution)/shard_map/ppermute | solution.py:43
  (15 other events, 117.3 us)
Sparse Core Ops, SparseCore 0:
  34.7 46.1 all-gather.2
  82.7 38.3 all-gather.4
